TPU v7x, 512 devices: a whole 4x4x16 slice. The times are simulated.
512 devices in a mesh: frame: 64 (over z_hi, x, y), ref: 8 (over z_lo, core).
Axes of the slice: x: 4, y: 4, z: 16 (z_hi: 4, z_lo: 4; z = z_hi * 4 + z_lo), core: 2. Of those that a mesh axis runs over, the one named last changes fastest.
Arguments:
- queries: bfloat16 [16384, 2048], P('frame', 'ref'), may hold values from -1.6953125 to 1.6953125
- keys: bfloat16 [16384, 2048], P('frame', 'ref'), may hold values from -1.6953125 to 1.6953125
- values: bfloat16 [16384, 2048], P('frame', 'ref'), may hold values from -6 to 6
- out_grad: bfloat16 [16384, 2048], P('frame', 'ref'), may hold values from -24 to 24
- ref_keys: bfloat16 [1024, 2048], P('ref'), may hold values from -1.6953125 to 1.6953125
- ref_values: bfloat16 [1024, 2048], P('ref'), may hold values from -6 to 6
- frame_weight: float32 [64], P('frame'), may hold values from 0.5 to 12, as said below
Outputs:
- grad_queries: bfloat16 [16384, 2048], P('frame', 'ref')
- grad_keys: bfloat16 [16384, 2048], P('frame', 'ref')
- grad_values: bfloat16 [16384, 2048], P('frame', 'ref')
- grad_ref_keys: float32 [1024, 2048], P('frame', 'ref')
- grad_ref_values: float32 [1024, 2048], P('frame', 'ref')
Inputs may be any that keep to these rules, and one draw needn't show every extreme that they name: `frame_weight`: positive loss weight of each frame.
All inputs are finite; a program needn't handle non-finite values.
Results may differ from a plain program's by a relative error of at most 0.005.
Values may be sent and summed in bfloat16 or wider, within the bound.
A program may use at most 64 MiB of HBM per device.

v0:
```python
import jax
import jax.numpy as jnp
from jax import lax
from jax.sharding import PartitionSpec as P

HEAD_DIM = 64


def head_grads(query_rows, key_self, value_self, grad_out, key_ref, value_ref, softmax_scale):
    length = query_rows.shape[0]
    all_keys = jnp.concatenate([key_self, key_ref], 0)
    all_values = jnp.concatenate([value_self, value_ref], 0)
    scores = jnp.dot(query_rows, all_keys.T, preferred_element_type=jnp.float32) * softmax_scale
    raised = jnp.exp(scores)
    shares = raised / jnp.sum(raised, axis=1, keepdims=True)
    shares_low = shares.astype(jnp.bfloat16)
    attended = jnp.dot(shares_low, all_values, preferred_element_type=jnp.float32)
    inner_term = jnp.sum(grad_out.astype(jnp.float32) * attended, axis=1, keepdims=True)
    grad_shares = jnp.dot(grad_out, all_values.T, preferred_element_type=jnp.float32)
    grad_scores = (shares * (grad_shares - inner_term)).astype(jnp.bfloat16)
    grad_query = jnp.dot(grad_scores, all_keys, preferred_element_type=jnp.float32) * softmax_scale
    grad_key = (
        jnp.dot(grad_scores[:, :length].T, query_rows, preferred_element_type=jnp.float32)
        * softmax_scale
    )
    grad_value = jnp.dot(shares_low[:, :length].T, grad_out, preferred_element_type=jnp.float32)
    return (grad_query, grad_key, grad_value, grad_scores[:, length:], shares_low[:, length:])


def ref_partial(ref_scores, ref_shares, query_rows, grad_out, softmax_scale):
    part_key = jnp.dot(ref_scores.T, query_rows, preferred_element_type=jnp.float32) * softmax_scale
    part_value = jnp.dot(ref_shares.T, grad_out, preferred_element_type=jnp.float32)
    return (part_key, part_value)


def frame_total(frame_weight):
    return lax.psum(frame_weight, "frame")


def per_device(queries, keys, values, out_grad, ref_keys, ref_values, frame_weight):
    head_size = HEAD_DIM
    width_dev = queries.shape[1]
    head_count = width_dev // head_size
    nframes = lax.axis_size("frame")
    softmax_scale = head_size ** (-0.5)
    ref_key_cols, ref_value_cols = (
        lax.all_to_all(ref_keys, "ref", split_axis=1, concat_axis=0, tiled=True),
        lax.all_to_all(ref_values, "ref", split_axis=1, concat_axis=0, tiled=True),
    )
    weight_here = frame_weight[0]
    factor = weight_here * (nframes / frame_total(frame_weight)[0])
    grads_query, grads_key, grads_value, ref_scores, ref_shares = ([], [], [], [], [])
    for head_index in range(head_count):
        low = head_index * head_size
        result = head_grads(
            queries[:, low : low + head_size],
            keys[:, low : low + head_size],
            values[:, low : low + head_size],
            out_grad[:, low : low + head_size],
            ref_key_cols[:, low : low + head_size],
            ref_value_cols[:, low : low + head_size],
            softmax_scale,
        )
        grads_query.append(result[0])
        grads_key.append(result[1])
        grads_value.append(result[2])
        ref_scores.append(result[3])
        ref_shares.append(result[4])
    key_parts = []
    value_parts = []
    for head_index in range(head_count):
        low = head_index * head_size
        part_key, part_value = ref_partial(
            ref_scores[head_index],
            ref_shares[head_index],
            queries[:, low : low + head_size],
            out_grad[:, low : low + head_size],
            softmax_scale,
        )
        key_parts.append(part_key)
        value_parts.append(part_value)
    whole_terms = factor * jnp.concatenate(key_parts + value_parts, 1)
    key_sum, value_sum = (
        lax.psum_scatter(whole_terms[:, :width_dev], "frame", scatter_dimension=0, tiled=True),
        lax.psum_scatter(whole_terms[:, width_dev:], "frame", scatter_dimension=0, tiled=True),
    )
    grad_queries = (factor * jnp.concatenate(grads_query, 1)).astype(jnp.bfloat16)
    grad_keys = (factor * jnp.concatenate(grads_key, 1)).astype(jnp.bfloat16)
    grad_values = (factor * jnp.concatenate(grads_value, 1)).astype(jnp.bfloat16)
    return (grad_queries, grad_keys, grad_values, key_sum, value_sum)


def solution(mesh):
    return jax.shard_map(
        per_device,
        mesh=mesh,
        in_specs=(
            P("frame", "ref"),
            P("frame", "ref"),
            P("frame", "ref"),
            P("frame", "ref"),
            P("ref", None),
            P("ref", None),
            P("frame"),
        ),
        out_specs=(
            P("frame", "ref"),
            P("frame", "ref"),
            P("frame", "ref"),
            P("frame", "ref"),
            P("frame", "ref"),
        ),
        check_vma=False,
    )
```

profile of v0, /device:TPU:6, one launch (start us, length us, event | category | flops | bytes accessed | tf_op | source)
XLA Modules:
  0.0 1148.9 jit_solution(681702791321305375)
XLA Ops:
  7.2 2.1 copy.43
  9.3 5.9 all-to-all-start
  15.2 1.0 copy.45
  16.2 14.3 %all-to-all-done = bf16[128,8,256]{0,2,1:T(8,128)(2,1)S(1)} async-done(((bf16[128,8,256]{0,2,1:T(8,128)(2,1)}), bf16[128,8,256]{0,2,1:T(8,128)(2,1)S(1)}, u32[]{:S(2)}, u32[]{:S(2)}) %all-to-all-start) | async-done | bytes 524320 | tf_op jit(solution)/shard_map/all_to_all | solution.py:47
  30.5 3.5 all-to-all-start.1
  34.1 206.6 %psum.7 = f32[1]{0:T(128)} all-reduce(f32[1]{0:T(128)} %param.13), channel_id=1, replica_groups=mesh['frame'=64,'ref'=8] {'frame'}, use_global_device_ids=true, to_apply=%region_0.0 | all-reduce | flops 1 | bytes 8 | tf_op jit(solution)/shard_map/psum | solution.py:37
  243.3 0.2 fusion.88
  243.5 0.2 fusion.89
  243.8 0.6 copy-done
  244.4 0.4 fusion.96
  245.0 0.3 fusion.16
  245.3 0.4 fusion.11
  245.7 0.5 fusion.93
  246.4 0.3 fusion.19
  246.7 0.4 fusion.8
  247.1 0.5 fusion.94
  247.7 0.3 fusion.18
  248.0 0.4 fusion.9
  248.4 0.5 fusion.95
  249.1 0.3 fusion.17
  249.4 0.4 fusion.10
  249.8 0.3 fusion.15
  250.1 0.4 fusion.14
  250.5 0.3 fusion.13
  250.8 0.4 fusion.12
  251.1 0.3 convolution_dynamic-update-slice_fusion.3
  251.4 0.4 convolution_dynamic-update-slice_fusion.2
  251.8 0.3 convolution_dynamic-update-slice_fusion.1
  252.1 0.4 convolution_dynamic-update-slice_fusion
  252.4 0.3 broadcast_multiply_fusion
  253.0 1.3 copy.58
  254.4 1.3 copy.56
  256.0 0.9 convolution_multiply_fusion.8
  256.9 1.8 convolution_multiply_fusion.9
  258.6 0.9 convolution_multiply_fusion.18
  259.6 1.3 convolution_multiply_fusion.10
  260.9 0.3 convolution_multiply_fusion.12
  261.3 0.3 convolution_multiply_fusion.14
  261.6 0.3 convolution_multiply_fusion.16
  262.2 0.8 copy.51
  262.9 1.1 fusion.41
  264.0 1.2 fusion.35
  265.2 1.1 fusion.37
  266.3 1.2 fusion.39
  267.5 0.8 copy.53
  268.3 0.8 copy.52
  269.0 431.4 %reduce-scatter.9.cloned.1.call-done = f32[16,256]{1,0:T(8,128)} async-done(((f32[1024,256]{1,0:T(8,128)}), f32[16,256]{1,0:T(8,128)}) %reduce-scatter.9.cloned.1.call-update) | async-done | bytes 16400
  700.5 441.5 %reduce-scatter.7.cloned.1.call-done = f32[16,256]{1,0:T(8,128)} async-done(((f32[1024,256]{1,0:T(8,128)}), f32[16,256]{1,0:T(8,128)}) %reduce-scatter.7.cloned.1.call-update) | async-done | bytes 16400
  (81 shorter events, 2.6 us)
Async XLA Ops:
  7.2 8.0 copy-start.16
  9.3 21.3 %all-to-all-start = ((bf16[128,8,256]{0,2,1:T(8,128)(2,1)}), bf16[128,8,256]{0,2,1:T(8,128)(2,1)S(1)}, u32[]{:S(2)}, u32[]{:S(2)}) async-start(bf16[128,8,256]{0,2,1:T(8,128)(2,1)} %bitcast.1), calls=%async_computation | async-start | bytes 1048576 | tf_op jit(solution)/shard_map/all_to_all | solution.py:47
  15.2 226.1 %copy-start.1 = (bf16[256,256]{1,0:T(8,128)(2,1)S(1)}, bf16[256,256]{1,0:T(8,128)(2,1)}, u32[]{:S(2)}) copy-start(bf16[256,256]{1,0:T(8,128)(2,1)} %param.10) | copy-start | bytes 393220
  15.2 227.3 %copy-start.17 = (bf16[256,256]{1,0:T(8,128)(2,1)S(1)}, bf16[256,256]{1,0:T(8,128)(2,1)}, u32[]{:S(2)}) copy-start(bf16[256,256]{1,0:T(8,128)(2,1)} %param.8) | copy-start | bytes 393220
  16.2 226.4 %copy-start.18 = (bf16[256,256]{1,0:T(8,128)(2,1)S(1)}, bf16[256,256]{1,0:T(8,128)(2,1)}, u32[]{:S(2)}) copy-start(bf16[256,256]{1,0:T(8,128)(2,1)} %param.9) | copy-start | bytes 393220
  30.5 212.5 %all-to-all-start.1 = ((bf16[128,8,256]{0,2,1:T(8,128)(2,1)}), bf16[128,8,256]{0,2,1:T(8,128)(2,1)S(1)}, u32[]{:S(2)}, u32[]{:S(2)}) async-start(bf16[128,8,256]{0,2,1:T(8,128)(2,1)} %bitcast.4), calls=%async_computation.1 | async-start | bytes 1048576 | tf_op jit(solution)/shard_map/all_to_all | solution.py:48
  34.0 666.4 %reduce-scatter.9.cloned.1.call-start = ((), (), s32[]{:S(2)}) async-start(), calls=%async_computation.5 | async-start | bytes 1064960
  242.7 1.1 copy-start.25
  242.7 3.0 copy-start.23
  242.7 4.4 copy-start.21
  242.7 5.7 copy-start.19
  243.5 0.9 copy-start
  243.8 1.1 copy-start.8
  243.8 1.9 copy-start.6
  245.0 6.1 copy-start.2
  245.7 4.1 copy-start.10
  246.4 5.7 copy-start.3
  247.7 4.1 copy-start.4
  248.4 2.1 copy-start.12
  249.1 2.4 copy-start.5
  249.8 1.3 copy-start.14
  254.3 1.4 copy-start.11
  254.4 887.7 %reduce-scatter.7.cloned.1.call-start = ((), (), s32[]{:S(2)}) async-start(), calls=%async_computation.4 | async-start | bytes 1064960
  254.4 4.2 copy-start.9
  254.4 4.2 copy-start.26
  256.8 4.0 copy-start.7
  256.9 4.1 copy-start.24
  259.6 1.6 copy-start.13
  259.6 1.7 copy-start.22
  259.6 2.0 copy-start.15
  259.6 2.0 copy-start.20
  261.2 0.8 copy-start.27
  261.2 0.9 copy-start.28
  261.2 0.9 copy-start.29
Sparse Core Ops, SparseCore 0:
  254.5 445.9 reduce-scatter.8
  704.1 437.9 reduce-scatter.6
where the time goes:
time: 1170 us; the launch traced here: 1150 us
  waiting for transfers between devices  887 us (76%)
  blocking collectives  207 us (18%)
  matrix products  17.7 us (2%)
  between operations  16 us (1%)
    unnamed x4, waiting for transfers between devices  873 us
    psum x1, blocking collectives, frame_total(): return lax.psum(frame_weight, 'frame')  207 us
  transfers between devices with their start and end apart: 4, of which 3 were waited for; matrix products, arithmetic and copies ran while one was open for 1% of the time, Pallas kernels for 0%

commit v1 on v0

v1 whole, which is shorter than its diff:
```python
import jax
import jax.numpy as jnp
from jax import lax
from jax.experimental import pallas as pl
from jax.experimental.pallas import tpu as pltpu
from jax.sharding import PartitionSpec as P

F32, BF = jnp.float32, jnp.bfloat16
MESH = pl.DeviceIdType.MESH
SCALE = 0.125
EXP2_SCALE = SCALE * 1.4426950408889634
SEQ, WIDTH, PAIR = 256, 256, 128
FRAMES = 64
KEY, VALUE = 0, 1


def dot(a, b):
    return lax.dot_general(a, b, (((1,), (0,)), ((), ())), preferred_element_type=F32)


def fold(a):
    return jnp.sum(a.reshape(-1, 8, a.shape[-1]), axis=0)


def split_heads(p, a, stacked, across):
    a = a[:, PAIR * p : PAIR * (p + 1)]
    low = lax.broadcasted_iota(jnp.int32, (SEQ, PAIR), 1) < 64
    zero = jnp.zeros((SEQ, PAIR), BF)
    stacked[p, 0:SEQ] = jnp.where(low, a, zero)
    stacked[p, SEQ:] = jnp.where(low, zero, a)
    turned = a.T
    top = lax.broadcasted_iota(jnp.int32, (PAIR, SEQ), 0) < 64
    zero = jnp.zeros((PAIR, SEQ), BF)
    across[p, :, 0:SEQ] = jnp.where(top, turned, zero)
    across[p, :, SEQ:] = jnp.where(top, zero, turned)


def kernel(
    q_in, k_in, v_in, d_in, rk_in, rv_in, w_in,
    gq_out, gk_out, gv_out, grk_out, grv_out,
    own, refs, stacked, across, raised, gshare, gscore, gq_t, gkv, result,
    part, got1, part2, got2, part3, got3, weights, weights_got, refout,
    loc_sem, out_sem, zs, zr, cs, cr, gs, gr, s1, r1, s2, r2, s3, r3, ws, wr,
):
    frame, ref = lax.axis_index("frame"), lax.axis_index("ref")
    zhi, x, y = frame // 16, (frame // 4) % 4, frame % 4
    zlo, core = ref // 2, ref % 2

    def at(dx=0, dy=0, dz=0, c=core):
        z = (zhi * 4 + zlo + dz + 16) % 16
        return (((z // 4) * 4 + (x + dx) % 4) * 4 + (y + dy) % 4, (z % 4) * 2 + c)

    near = [at(c=1 - core)]
    near += [at(dz=dz, c=c) for dz in (1, -1, 2, -2) for c in (0, 1)]
    near += [at(dx=o) for o in (1, 2, 3)] + [at(dy=o) for o in (1, 2, 3)]
    near += [at(dz=4 * o) for o in (1, 2, 3)]
    barrier = pltpu.get_barrier_semaphore()
    for device in near:
        pl.semaphore_signal(barrier, inc=1, device_id=device, device_id_type=MESH)

    def columns(r, h):
        return pl.ds(pl.multiple_of(r * WIDTH + h * PAIR, PAIR), PAIR)

    local = []
    for i, a in enumerate((q_in, d_in, k_in, v_in)):
        local.append(pltpu.make_async_copy(a, own.at[i], loc_sem.at[i]))
    ref_in = (rk_in, rv_in)
    local_ref = [
        [pltpu.make_async_copy(ref_in[t].at[:, :, columns(ref, h)], refs.at[t, h, 0, core], loc_sem.at[4 + 2 * h + t]) for t in (0, 1)]
        for h in (0, 1)
    ]
    for copy in local + local_ref[0] + local_ref[1]:
        copy.start()
    weight = w_in[0]
    weights[0] = jnp.full((8, 128), weight, F32)
    pl.semaphore_wait(barrier, len(near))

    sent = []

    def send(src, dst, send_sem, recv_sem, device):
        copy = pltpu.make_async_remote_copy(src, dst, send_sem, recv_sem, device_id=device, device_id_type=MESH)
        copy.start()
        sent.append(copy)

    def arrived(region, sem, any_send_sem):
        pltpu.make_async_remote_copy(region, region, any_send_sem, sem, device_id=at(dx=1), device_id_type=MESH).wait_recv()

    quarter = (x, y)
    for h in (0, 1):
        for t in (0, 1):
            for i, dz in enumerate((1, -1, 2 if t == 0 else -2)):
                slot = (3, 1, 2)[i]
                for c in (0, 1):
                    target = at(dz=dz, c=c)
                    here = ref_in[t].at[quarter[t], :, columns(target[1], h)]
                    send(here, refs.at[t, h, slot, core, quarter[t]], zs.at[h, t, i, c], zr.at[h, t], target)
        for t in (0, 1):
            here = ref_in[t].at[:, :, columns(zlo * 2 + 1 - core, h)]
            send(here, refs.at[t, h, 0, core], cs.at[h, t], cr.at[h, t], at(c=1 - core))
    for o in (1, 2, 3):
        send(weights.at[0], weights_got.at[0, o - 1], ws.at[0, o - 1], wr.at[0, o - 1], at(dx=o))

    def gather_planes(h):
        for t in (0, 1):
            mine = refs.at[t, h, 1:4, :, quarter[t]]
            arrived(mine, zr.at[h, t], zs.at[0, 0, 0, 0])
            for o in (1, 2, 3):
                send(mine, mine, gs.at[h, t, o - 1], gr.at[h, t, o - 1], at(dx=o) if t == 0 else at(dy=o))

    def scores(p, j, keys, values):
        e = jnp.exp2(dot(keys, across[0, p]) * EXP2_SCALE)
        g = dot(values, across[1, p])
        raised[p, j] = e
        gshare[p, j] = g
        return fold(e), fold(e * g)

    def ref_chunk(t, p, s):
        return refs[t, p, s].reshape(SEQ, PAIR)

    def own_chunk(i, p):
        return own[i, :, PAIR * p : PAIR * (p + 1)]

    local[0].wait()
    local[1].wait()
    for p in (0, 1):
        split_heads(p, own[0], stacked.at[0], across.at[0])
        split_heads(p, own[1], stacked.at[1], across.at[1])
    gather_planes(0)
    local[2].wait()
    local[3].wait()
    totals = [None, None]

    def add(p, more):
        totals[p] = more if totals[p] is None else (totals[p][0] + more[0], totals[p][1] + more[1])

    add(0, scores(0, 4, own_chunk(2, 0), own_chunk(3, 0)))
    gather_planes(1)
    add(1, scores(1, 4, own_chunk(2, 1), own_chunk(3, 1)))
    for h in (0, 1):
        for t in (0, 1):
            local_ref[h][t].wait()
            arrived(refs.at[t, h, 0, 1 - core], cr.at[h, t], cs.at[0, 0])
        add(h, scores(h, 0, ref_chunk(0, h, 0), ref_chunk(1, h, 0)))

    def weight_stage(stage):
        for o in (1, 2, 3):
            arrived(weights_got.at[stage, o - 1], wr.at[stage, o - 1], ws.at[0, 0])
        weights[stage + 1] = weights[stage] + weights_got[stage, 0] + weights_got[stage, 1] + weights_got[stage, 2]
        if stage < 2:
            for o in (1, 2, 3):
                target = at(dy=o) if stage == 0 else at(dz=4 * o)
                send(weights.at[stage + 1], weights_got.at[stage + 1, o - 1], ws.at[stage + 1, o - 1], wr.at[stage + 1, o - 1], target)

    weight_stage(0)

    def shares(p, j, norm):
        share = raised[p, j] * norm[0]
        score = (share * (gshare[p, j] - norm[1])).astype(BF)
        gscore[p, j] = score
        return dot(score, stacked[0, p]), dot(share.astype(BF), stacked[1, p])

    norms = [None, None]

    def partial_grads(p):
        for t in (0, 1):
            for o in (1, 2, 3):
                arrived(refs.at[t, p, 1:4, :, (quarter[t] + 4 - o) % 4], gr.at[p, t, o - 1], gs.at[0, 0, 0])
        for s in (1, 2, 3):
            add(p, scores(p, s, ref_chunk(0, p, s), ref_chunk(1, p, s)))
        norm = 1.0 / jnp.sum(totals[p][0], axis=0, keepdims=True)
        norms[p] = (norm, jnp.sum(totals[p][1], axis=0, keepdims=True) * norm)
        for s in range(4):
            for t, grad in enumerate(shares(p, s, norms[p])):
                part[t, p, s] = (grad * weight).astype(BF).reshape(4, 4, 16, PAIR)
        for o in (1, 2, 3):
            send(part.at[0, p, :, (x + o) % 4], got1.at[0, p, o - 1], s1.at[0, p, o - 1], r1.at[0, p, o - 1], at(dx=o))
            send(part.at[1, p, :, :, (y + o) % 4], got1.at[1, p, o - 1], s1.at[1, p, o - 1], r1.at[1, p, o - 1], at(dy=o))

    def total(first, got):
        return first.astype(F32) + got[0].astype(F32) + got[1].astype(F32) + got[2].astype(F32)

    def second_stage(p):
        for t in (0, 1):
            for o in (1, 2, 3):
                arrived(got1.at[t, p, o - 1], r1.at[t, p, o - 1], s1.at[0, 0, 0])
            mine = part[0, p, :, x] if t == 0 else part[1, p, :, :, y]
            part2[t, p] = total(mine, got1.at[t, p]).astype(BF)
            place, device = (y, lambda o: at(dy=o)) if t == 0 else (x, lambda o: at(dx=o))
            for o in (1, 2, 3):
                send(part2.at[t, p, :, (place + o) % 4], got2.at[t, p, o - 1], s2.at[t, p, o - 1], r2.at[t, p, o - 1], device(o))

    def third_stage(p):
        for t in (0, 1):
            for o in (1, 2, 3):
                arrived(got2.at[t, p, o - 1], r2.at[t, p, o - 1], s2.at[0, 0, 0])
            part3[t, p] = total(part2[t, p, :, y if t == 0 else x], got2.at[t, p]).astype(BF)
            for o in (1, 2, 3):
                slot = (zhi + o - zlo + 4) % 4
                send(part3.at[t, p, slot], got3.at[t, p, o - 1], s3.at[t, p, o - 1], r3.at[t, p, o - 1], at(dz=4 * o))

    def frame_grads(p):
        gk, gv = shares(p, 4, norms[p])
        gkv[0, p] = gk
        gkv[1, p] = gv
        sums = [None, None]
        for j in range(5):
            turned = (own_chunk(2, p) if j == 4 else ref_chunk(0, p, j)).T
            for a in (0, 1):
                more = dot(turned[64 * a : 64 * (a + 1)], gscore[p, j, :, SEQ * a : SEQ * (a + 1)])
                sums[a] = more if sums[a] is None else sums[a] + more
        gq_t[p, 0:64] = sums[0]
        gq_t[p, 64:128] = sums[1]

    partial_grads(0)
    partial_grads(1)
    second_stage(0)
    weight_stage(1)
    frame_grads(0)
    second_stage(1)
    third_stage(0)
    frame_grads(1)
    third_stage(1)

    weight_stage(2)
    factor = FRAMES / weights[3, 0:1, 0:1]
    own_factor = weight * factor
    for p in (0, 1):
        cols = slice(PAIR * p, PAIR * (p + 1))
        result[0, :, cols] = (gq_t[p].T * (own_factor * SCALE)).astype(BF)
        result[1, :, cols] = (gkv[0, p] * (own_factor * SCALE)).astype(BF)
        result[2, :, cols] = (gkv[1, p] * own_factor).astype(BF)
    out = [pltpu.make_async_copy(result.at[i], a, out_sem.at[i]) for i, a in enumerate((gq_out, gk_out, gv_out))]
    for copy in out:
        copy.start()
    for p in (0, 1):
        for t in (0, 1):
            for o in (1, 2, 3):
                arrived(got3.at[t, p, o - 1], r3.at[t, p, o - 1], s3.at[0, 0, 0])
            mine = part3[t, p, (zhi - zlo + 4) % 4]
            refout[t, :, PAIR * p : PAIR * (p + 1)] = total(mine, got3.at[t, p]) * (factor * (SCALE if t == 0 else 1.0))
    for t, a in enumerate((grk_out, grv_out)):
        out.append(pltpu.make_async_copy(refout.at[t], a, out_sem.at[3 + t]))
        out[-1].start()
    for copy in sent:
        copy.wait_send()
    for copy in out:
        copy.wait()


def per_device(queries, keys, values, out_grad, ref_keys, ref_values, frame_weight):
    hbm = pl.BlockSpec(memory_space=pl.ANY)
    shape = jax.ShapeDtypeStruct
    vmem, dma = pltpu.VMEM, pltpu.SemaphoreType.DMA
    return pl.pallas_call(
        kernel,
        name="joint_attention_grads",
        out_shape=(
            shape((SEQ, WIDTH), BF),
            shape((SEQ, WIDTH), BF),
            shape((SEQ, WIDTH), BF),
            shape((16, WIDTH), F32),
            shape((16, WIDTH), F32),
        ),
        in_specs=[hbm] * 6 + [pl.BlockSpec(memory_space=pltpu.SMEM)],
        out_specs=[hbm] * 5,
        scratch_shapes=[
            vmem((4, SEQ, WIDTH), BF),
            vmem((2, 2, 4, 2, 4, 32, PAIR), BF),
            vmem((2, 2, 2 * SEQ, PAIR), BF),
            vmem((2, 2, PAIR, 2 * SEQ), BF),
            vmem((2, 5, SEQ, 2 * SEQ), F32),
            vmem((2, 5, SEQ, 2 * SEQ), F32),
            vmem((2, 5, SEQ, 2 * SEQ), BF),
            vmem((2, PAIR, SEQ), F32),
            vmem((2, 2, SEQ, PAIR), F32),
            vmem((3, SEQ, WIDTH), BF),
            vmem((2, 2, 4, 4, 4, 16, PAIR), BF),
            vmem((2, 2, 3, 4, 4, 16, PAIR), BF),
            vmem((2, 2, 4, 4, 16, PAIR), BF),
            vmem((2, 2, 3, 4, 16, PAIR), BF),
            vmem((2, 2, 4, 16, PAIR), BF),
            vmem((2, 2, 3, 16, PAIR), BF),
            vmem((4, 8, 128), F32),
            vmem((3, 3, 8, 128), F32),
            vmem((2, 16, WIDTH), F32),
            dma((8,)),
            dma((5,)),
            dma((2, 2, 3, 2)),
            dma((2, 2)),
            dma((2, 2)),
            dma((2, 2)),
            dma((2, 2, 3)),
            dma((2, 2, 3)),
            dma((2, 2, 3)),
            dma((2, 2, 3)),
            dma((2, 2, 3)),
            dma((2, 2, 3)),
            dma((2, 2, 3)),
            dma((2, 2, 3)),
            dma((3, 3)),
            dma((3, 3)),
        ],
        compiler_params=pltpu.CompilerParams(
            collective_id=0, has_side_effects=True, vmem_limit_bytes=44 * 2**20
        ),
    )(
        queries,
        keys,
        values,
        out_grad,
        ref_keys.reshape(4, 32, -1),
        ref_values.reshape(4, 32, -1),
        frame_weight,
    )


def solution(mesh):
    tokens = P("frame", "ref")
    return jax.shard_map(
        per_device,
        mesh=mesh,
        in_specs=(tokens, tokens, tokens, tokens, P("ref", None), P("ref", None), P("frame")),
        out_specs=(tokens,) * 5,
        check_vma=False,
    )
```

time: 1170 us -> 57.4 us (0.05); the launches traced: 1150 us -> 56.9 us
  waiting for transfers between devices: 887 us -> 0 us
  blocking collectives: 207 us -> 0 us
  Pallas kernels: 0 us -> 46.7 us
  matrix products: 17.7 us -> 0 us
  between operations: 16 us -> 1.3 us
    unnamed x4 -> x0, waiting for transfers between devices: 873 us -> none
    psum x1 -> x0, blocking collectives: 207 us -> none  [frame_total(): return lax.psum(frame_weight, 'frame')]
    pallas_call x0 -> x1, Pallas kernels: none -> 46.7 us  [per_device(): pl.pallas_call(kernel, name='joint_attention_grads', out_shape=(shape((SE...]
    dot_general x32 -> x0, matrix products: 17.7 us -> none  [the longest x4 4.53 us: head_grads(): jnp.dot(shares_low[:, :length].T, grad_out, preferred_element_type=jnp.fl...]
    all_to_all x2 -> x0, waiting for transfers between devices: 14.3 us -> none  [the longest x1 14.3 us: per_device(): lax.all_to_all(ref_keys, 'ref', split_axis=1, concat_axis=0, tiled=True)]
  transfers between devices with their start and end apart: 4 -> 0, of which waited for: 3 -> 0; matrix products, arithmetic and copies ran while one was open for 1% -> 0% of each run, Pallas kernels for 0% -> 0%
where the time goes in v1:
time: 57.4 us; the launch traced here: 56.9 us
  Pallas kernels  46.7 us (81%)
  local copies, waits for them, and re-layouts  8.87 us (15%)
  between operations  1.3 us (2%)
    pallas_call x1, Pallas kernels, per_device(): pl.pallas_call(kernel, name='joint_attention_grads', out_shape=(shape((SE...  46.7 us
    unnamed x17, local copies, waits for them, and re-layouts  8.87 us

profile of v1, /device:TPU:6, one launch (start us, length us, event | category | flops | bytes accessed | tf_op | source)
XLA Modules:
  0.0 56.9 jit_solution(9682199048641089808)
XLA Ops:
  1.3 0.0 copy-start
  1.3 1.0 %copy-done = bf16[128,2048]{1,0:T(8,128)(2,1)S(1)} copy-done((bf16[128,2048]{1,0:T(8,128)(2,1)S(1)}, bf16[128,2048]{1,0:T(8,128)(2,1)}, u32[]{:S(2)}) %copy-start) | copy-done | bytes 524312
  2.3 0.0 copy-start.1
  2.3 1.0 %copy-done.1 = bf16[128,2048]{1,0:T(8,128)(2,1)S(1)} copy-done((bf16[128,2048]{1,0:T(8,128)(2,1)S(1)}, bf16[128,2048]{1,0:T(8,128)(2,1)}, u32[]{:S(2)}) %copy-start.1) | copy-done | bytes 524312
  3.4 0.0 copy-start.2
  3.4 0.9 %copy-done.2 = bf16[256,256]{1,0:T(8,128)(2,1)S(1)} copy-done((bf16[256,256]{1,0:T(8,128)(2,1)S(1)}, bf16[256,256]{1,0:T(8,128)(2,1)}, u32[]{:S(2)}) %copy-start.2) | copy-done | bytes 131096
  4.3 0.0 copy-start.3
  4.3 0.9 %copy-done.3 = bf16[256,256]{1,0:T(8,128)(2,1)S(1)} copy-done((bf16[256,256]{1,0:T(8,128)(2,1)S(1)}, bf16[256,256]{1,0:T(8,128)(2,1)}, u32[]{:S(2)}) %copy-start.3) | copy-done | bytes 131096
  5.2 0.0 copy-start.4
  5.2 0.9 %copy-done.4 = bf16[256,256]{1,0:T(8,128)(2,1)S(1)} copy-done((bf16[256,256]{1,0:T(8,128)(2,1)S(1)}, bf16[256,256]{1,0:T(8,128)(2,1)}, u32[]{:S(2)}) %copy-start.4) | copy-done | bytes 131096
  6.1 0.0 copy-start.5
  6.1 0.9 %copy-done.5 = bf16[256,256]{1,0:T(8,128)(2,1)S(1)} copy-done((bf16[256,256]{1,0:T(8,128)(2,1)S(1)}, bf16[256,256]{1,0:T(8,128)(2,1)}, u32[]{:S(2)}) %copy-start.5) | copy-done | bytes 131096
  7.0 46.7 %joint_attention_grads.1 = (bf16[256,256]{1,0:T(8,128)(2,1)S(1)}, bf16[256,256]{1,0:T(8,128)(2,1)S(1)}, bf16[256,256]{1,0:T(8,128)(2,1)S(1)}, f32[16,256]{1,0:T(8,128)S(1)}, f32[16,256]{1,0:T(8,128)S(1)}) custom-call(bf16[256,256]{1,0:T(8,128)(2,1)S(1)} %copy-done.2, bf16[256,256]{1,0:T(8,128)(2,1)S(1)} %copy-done.3, bf16[256,256]{1,0:T(8,128)(2,1)S(1)} %copy-done.4, ...), custom_call_target="tpu_custom_call" | custom-call | tf_op jit(solution)/shard_map/joint_attention_grads/pallas_call | solution.py:254
  53.7 0.7 %copy.18 = bf16[256,256]{1,0:T(8,128)(2,1)} copy(bf16[256,256]{1,0:T(8,128)(2,1)S(1)} %get-tuple-element.10) | data formatting | bytes 262144
  54.3 0.7 %copy.19 = bf16[256,256]{1,0:T(8,128)(2,1)} copy(bf16[256,256]{1,0:T(8,128)(2,1)S(1)} %get-tuple-element.11) | data formatting | bytes 262144
  55.0 0.7 %copy.20 = bf16[256,256]{1,0:T(8,128)(2,1)} copy(bf16[256,256]{1,0:T(8,128)(2,1)S(1)} %get-tuple-element.12) | data formatting | bytes 262144
  55.6 0.6 %copy.21 = f32[16,256]{1,0:T(8,128)} copy(f32[16,256]{1,0:T(8,128)S(1)} %get-tuple-element.13) | data formatting | bytes 32768
  56.3 0.6 %copy.22 = f32[16,256]{1,0:T(8,128)} copy(f32[16,256]{1,0:T(8,128)S(1)} %get-tuple-element.14) | data formatting | bytes 32768
Async XLA Ops:
  1.3 1.0 %copy-start = (bf16[128,2048]{1,0:T(8,128)(2,1)S(1)}, bf16[128,2048]{1,0:T(8,128)(2,1)}, u32[]{:S(2)}) copy-start(bf16[128,2048]{1,0:T(8,128)(2,1)} %param.11) | copy-start | bytes 1572868
  2.3 1.0 %copy-start.1 = (bf16[128,2048]{1,0:T(8,128)(2,1)S(1)}, bf16[128,2048]{1,0:T(8,128)(2,1)}, u32[]{:S(2)}) copy-start(bf16[128,2048]{1,0:T(8,128)(2,1)} %param.12) | copy-start | bytes 1572868
  3.4 0.9 %copy-start.2 = (bf16[256,256]{1,0:T(8,128)(2,1)S(1)}, bf16[256,256]{1,0:T(8,128)(2,1)}, u32[]{:S(2)}) copy-start(bf16[256,256]{1,0:T(8,128)(2,1)} %q_in.1) | copy-start | bytes 393220
  4.3 0.9 %copy-start.3 = (bf16[256,256]{1,0:T(8,128)(2,1)S(1)}, bf16[256,256]{1,0:T(8,128)(2,1)}, u32[]{:S(2)}) copy-start(bf16[256,256]{1,0:T(8,128)(2,1)} %k_in.1) | copy-start | bytes 393220
  5.2 0.9 %copy-start.4 = (bf16[256,256]{1,0:T(8,128)(2,1)S(1)}, bf16[256,256]{1,0:T(8,128)(2,1)}, u32[]{:S(2)}) copy-start(bf16[256,256]{1,0:T(8,128)(2,1)} %v_in.1) | copy-start | bytes 393220
  6.1 0.9 %copy-start.5 = (bf16[256,256]{1,0:T(8,128)(2,1)S(1)}, bf16[256,256]{1,0:T(8,128)(2,1)}, u32[]{:S(2)}) copy-start(bf16[256,256]{1,0:T(8,128)(2,1)} %d_in.1) | copy-start | bytes 393220

commit v2 on v1

v2 whole, which is shorter than its diff:
```python
import jax
import jax.numpy as jnp
from jax import lax
from jax.experimental import pallas as pl
from jax.experimental.pallas import tpu as pltpu
from jax.sharding import PartitionSpec as P

F32, BF = jnp.float32, jnp.bfloat16
MESH = pl.DeviceIdType.MESH
SCALE = 0.125
EXP2_SCALE = SCALE * 1.4426950408889634
SEQ, WIDTH, PAIR = 256, 256, 128
FRAMES = 64
KEY, VALUE = 0, 1


def dot(a, b):
    return lax.dot_general(a, b, (((1,), (0,)), ((), ())), preferred_element_type=F32)


def fold(a):
    return jnp.sum(a.reshape(-1, 8, a.shape[-1]), axis=0)


def split_heads(p, a, stacked, across):
    a = a[:, PAIR * p : PAIR * (p + 1)]
    low = lax.broadcasted_iota(jnp.int32, (SEQ, PAIR), 1) < 64
    zero = jnp.zeros((SEQ, PAIR), BF)
    stacked[p, 0:SEQ] = jnp.where(low, a, zero)
    stacked[p, SEQ:] = jnp.where(low, zero, a)
    turned = a.T
    top = lax.broadcasted_iota(jnp.int32, (PAIR, SEQ), 0) < 64
    zero = jnp.zeros((PAIR, SEQ), BF)
    across[p, :, 0:SEQ] = jnp.where(top, turned, zero)
    across[p, :, SEQ:] = jnp.where(top, zero, turned)


def kernel(
    q_in, k_in, v_in, d_in, rk_in, rv_in, w_in,
    gq_out, gk_out, gv_out, grk_out, grv_out,
    own, refs, stacked, across, raised, gshare, gscore, gq_t, gkv, result,
    part, got1, part2, got2, part3, got3, own_weight, weights, weights_got, refout,
    loc_sem, out_sem, zs, zr, cs, cr, gs, gr, s1, r1, s2, r2, s3, r3, ws, wr, hop_sem,
):
    frame, ref = lax.axis_index("frame"), lax.axis_index("ref")
    zhi, x, y = frame // 16, (frame // 4) % 4, frame % 4
    zlo, core = ref // 2, ref % 2

    def at(dx=0, dy=0, dz=0, c=core):
        z = (zhi * 4 + zlo + dz + 16) % 16
        return (((z // 4) * 4 + (x + dx) % 4) * 4 + (y + dy) % 4, (z % 4) * 2 + c)

    def signal(sem, device):
        pl.semaphore_signal(sem, inc=1, device_id=device, device_id_type=MESH)

    near = [at(c=1 - core)]
    near += [at(dz=dz, c=c) for dz in (1, -1, 2, -2) for c in (0, 1)]
    near += [at(dx=o) for o in (1, 2, 3)] + [at(dy=o) for o in (1, 2, 3)]
    barrier = pltpu.get_barrier_semaphore()
    for device in near:
        signal(barrier, device)

    def columns(r, h):
        return pl.ds(pl.multiple_of(r * WIDTH + h * PAIR, PAIR), PAIR)

    ref_in = (rk_in, rv_in)
    local = [pltpu.make_async_copy(a, own.at[i], loc_sem.at[i]) for i, a in enumerate((q_in, d_in, k_in, v_in))]
    local_ref = [
        [pltpu.make_async_copy(ref_in[t].at[:, :, columns(ref, h)], refs.at[t, h, 0, core], loc_sem.at[4 + 2 * h + t]) for t in (0, 1)]
        for h in (0, 1)
    ]
    weight_copy = pltpu.make_async_copy(w_in, own_weight, loc_sem.at[8])
    for copy in [weight_copy] + local + local_ref[0] + local_ref[1]:
        copy.start()
    pl.semaphore_wait(barrier, len(near))
    for dz in (2, -2):
        signal(hop_sem.at[0], at(dz=dz))

    sent = []

    def send(src, dst, send_sem, recv_sem, device):
        copy = pltpu.make_async_remote_copy(src, dst, send_sem, recv_sem, device_id=device, device_id_type=MESH)
        copy.start()
        sent.append(copy)

    def arrived(region, sem, any_send_sem):
        pltpu.make_async_remote_copy(region, region, any_send_sem, sem, device_id=at(dx=1), device_id_type=MESH).wait_recv()

    quarter = (x, y)
    groups = ((1, 3), (3, 4))
    for h in (0, 1):
        for group, hops in enumerate((((1, 2), (-1, 1)), ((2, 3),))):
            for t in (0, 1):
                for dz, place in hops:
                    for c in (0, 1):
                        target = at(dz=-dz if place == 3 and t == 1 else dz, c=c)
                        here = ref_in[t].at[quarter[t], :, columns(target[1], h)]
                        send(here, refs.at[t, h, place, core, quarter[t]], zs.at[h, t, place - 1, c], zr.at[h, t, group], target)
    weight_copy.wait()
    weights[0] = jnp.broadcast_to(own_weight[...], (8, 128))
    for h in (0, 1):
        for t in (0, 1):
            here = ref_in[t].at[:, :, columns(zlo * 2 + 1 - core, h)]
            send(here, refs.at[t, h, 0, core], cs.at[h, t], cr.at[h, t], at(c=1 - core))
    for o in (1, 2, 3):
        send(weights.at[0], weights_got.at[0, o - 1], ws.at[0, o - 1], wr.at[0, o - 1], at(dx=o))

    def gather_planes(h, group):
        first, last = groups[group]
        for t in (0, 1):
            mine = refs.at[t, h, first:last, :, quarter[t]]
            arrived(mine, zr.at[h, t, group], zs.at[0, 0, 0, 0])
            for o in (1, 2, 3):
                send(mine, mine, gs.at[h, t, group, o - 1], gr.at[h, t, group, o - 1], at(dx=o) if t == 0 else at(dy=o))

    def wait_planes(h, group):
        first, last = groups[group]
        for t in (0, 1):
            for o in (1, 2, 3):
                arrived(refs.at[t, h, first:last, :, (quarter[t] + 4 - o) % 4], gr.at[h, t, group, o - 1], gs.at[0, 0, 0, 0])

    totals = [None, None]

    def scores(p, j, keys, values):
        e = jnp.exp2(dot(keys, across[0, p]) * EXP2_SCALE)
        g = dot(values, across[1, p])
        raised[p, j] = e
        gshare[p, j] = g
        more = (fold(e), fold(e * g))
        totals[p] = more if totals[p] is None else (totals[p][0] + more[0], totals[p][1] + more[1])

    def ref_chunk(t, p, s):
        return refs[t, p, s].reshape(SEQ, PAIR)

    def ref_scores(p, s):
        scores(p, s, ref_chunk(0, p, s), ref_chunk(1, p, s))

    def own_chunk(i, p):
        return own[i, :, PAIR * p : PAIR * (p + 1)]

    def weight_stage(stage):
        for o in (1, 2, 3):
            arrived(weights_got.at[stage, o - 1], wr.at[stage, o - 1], ws.at[0, 0])
        weights[stage + 1] = weights[stage] + weights_got[stage, 0] + weights_got[stage, 1] + weights_got[stage, 2]
        if stage < 2:
            for o in (1, 2, 3):
                target = at(dy=o) if stage == 0 else at(dz=4 * o)
                send(weights.at[stage + 1], weights_got.at[stage + 1, o - 1], ws.at[stage + 1, o - 1], wr.at[stage + 1, o - 1], target)

    local[0].wait()
    local[1].wait()
    for p in (0, 1):
        split_heads(p, own[0], stacked.at[0], across.at[0])
        split_heads(p, own[1], stacked.at[1], across.at[1])
    gather_planes(0, 0)
    local[2].wait()
    local[3].wait()
    scores(0, 4, own_chunk(2, 0), own_chunk(3, 0))
    gather_planes(0, 1)
    scores(1, 4, own_chunk(2, 1), own_chunk(3, 1))
    gather_planes(1, 0)
    gather_planes(1, 1)
    pl.semaphore_wait(hop_sem.at[0], 2)
    for dz in (4, -4):
        signal(hop_sem.at[1], at(dz=dz))
    weight_stage(0)
    for h in (0, 1):
        for t in (0, 1):
            local_ref[h][t].wait()
            arrived(refs.at[t, h, 0, 1 - core], cr.at[h, t], cs.at[0, 0])
        ref_scores(h, 0)

    def shares(p, j, norm):
        share = raised[p, j] * norm[0]
        score = (share * (gshare[p, j] - norm[1])).astype(BF)
        gscore[p, j] = score
        return dot(score, stacked[0, p]), dot(share.astype(BF), stacked[1, p])

    norms = [None, None]

    def normalise(p):
        norm = 1.0 / jnp.sum(totals[p][0], axis=0, keepdims=True)
        norms[p] = (norm, jnp.sum(totals[p][1], axis=0, keepdims=True) * norm)

    order = (2, 1, 3, 0)
    parts = ((0, 1), (1, 4))
    weight = own_weight[...]

    def first_stage(p, group):
        first, last = parts[group]
        for i in range(first, last):
            step = (zhi + order[i] - zlo + 4) % 4
            place = step + (step // 2) * (5 - 2 * step)
            for t, grad in enumerate(shares(p, place, norms[p])):
                part[t, p, i] = (grad * weight).astype(BF).reshape(4, 4, 16, PAIR)
        for o in (1, 2, 3):
            for t in (0, 1):
                here = part.at[0, p, first:last, (x + o) % 4] if t == 0 else part.at[1, p, first:last, :, (y + o) % 4]
                send(here, got1.at[t, p, o - 1, first:last], s1.at[t, p, group, o - 1], r1.at[t, p, group, o - 1], at(dx=o) if t == 0 else at(dy=o))

    def total(first, got):
        return first.astype(F32) + got[0].astype(F32) + got[1].astype(F32) + got[2].astype(F32)

    def second_stage(p, group):
        first, last = parts[group]
        for t in (0, 1):
            for o in (1, 2, 3):
                arrived(got1.at[t, p, o - 1, first:last], r1.at[t, p, group, o - 1], s1.at[0, 0, 0, 0])
            mine = part[0, p, first:last, x] if t == 0 else part[1, p, first:last, :, y]
            part2[t, p, first:last] = total(mine, got1[t, p, :, first:last]).astype(BF)
            for o in (1, 2, 3):
                here = part2.at[t, p, first:last, (y + o) % 4 if t == 0 else (x + o) % 4]
                send(here, got2.at[t, p, o - 1, first:last], s2.at[t, p, group, o - 1], r2.at[t, p, group, o - 1], at(dy=o) if t == 0 else at(dx=o))

    def third_stage(p, group):
        first, last = parts[group]
        for t in (0, 1):
            for o in (1, 2, 3):
                arrived(got2.at[t, p, o - 1, first:last], r2.at[t, p, group, o - 1], s2.at[0, 0, 0, 0])
            part3[p, first:last, t] = total(part2[t, p, first:last, y if t == 0 else x], got2[t, p, :, first:last]).astype(BF)
        for i in range(first, min(last, 3)):
            send(part3.at[p, i], got3.at[p, i], s3.at[p, i], r3.at[p, i], at(dz=4 * order[i]))

    def frame_grads(p):
        gk, gv = shares(p, 4, norms[p])
        gkv[0, p] = gk
        gkv[1, p] = gv
        sums = [None, None]
        for j in range(5):
            turned = (own_chunk(2, p) if j == 4 else ref_chunk(0, p, j)).T
            for a in (0, 1):
                more = dot(turned[64 * a : 64 * (a + 1)], gscore[p, j, :, SEQ * a : SEQ * (a + 1)])
                sums[a] = more if sums[a] is None else sums[a] + more
        gq_t[p, 0:64] = sums[0]
        gq_t[p, 64:128] = sums[1]

    wait_planes(0, 0)
    ref_scores(0, 1)
    ref_scores(0, 2)
    wait_planes(0, 1)
    ref_scores(0, 3)
    normalise(0)
    first_stage(0, 0)
    first_stage(0, 1)
    pl.semaphore_wait(hop_sem.at[1], 2)
    weight_stage(1)
    wait_planes(1, 0)
    ref_scores(1, 1)
    ref_scores(1, 2)
    wait_planes(1, 1)
    ref_scores(1, 3)
    normalise(1)
    first_stage(1, 0)
    first_stage(1, 1)
    second_stage(0, 0)
    second_stage(0, 1)
    second_stage(1, 0)
    third_stage(0, 0)
    third_stage(0, 1)
    second_stage(1, 1)
    third_stage(1, 0)
    third_stage(1, 1)
    frame_grads(0)
    frame_grads(1)
    weight_stage(2)
    factor = FRAMES / weights[3, 0:1, 0:1]
    own_factor = weight * factor
    for p in (0, 1):
        cols = slice(PAIR * p, PAIR * (p + 1))
        result[0, :, cols] = (gq_t[p].T * (own_factor * SCALE)).astype(BF)
        result[1, :, cols] = (gkv[0, p] * (own_factor * SCALE)).astype(BF)
        result[2, :, cols] = (gkv[1, p] * own_factor).astype(BF)
    out = [pltpu.make_async_copy(result.at[i], a, out_sem.at[i]) for i, a in enumerate((gq_out, gk_out, gv_out))]
    for copy in out:
        copy.start()
    for copy in sent:
        copy.wait_send()
    for p in (0, 1):
        for i in range(3):
            arrived(got3.at[p, i], r3.at[p, i], s3.at[0, 0])
        sums = total(part3[p, 3], got3[p])
        for t in (0, 1):
            refout[t, :, PAIR * p : PAIR * (p + 1)] = sums[t] * (factor * (SCALE if t == 0 else 1.0))
    for t, a in enumerate((grk_out, grv_out)):
        out.append(pltpu.make_async_copy(refout.at[t], a, out_sem.at[3 + t]))
        out[-1].start()
    for copy in out:
        copy.wait()


def hand_on(*refs):
    ins, outs, held, sem_in, sem_out = refs[0:5], refs[5:10], refs[10:15], refs[15], refs[16]
    into = [pltpu.make_async_copy(ins[i], held[i], sem_in.at[i]) for i in range(5)]
    out = [pltpu.make_async_copy(held[i], outs[i], sem_out.at[i]) for i in range(5)]
    for copy in into:
        copy.start()
    for i in range(5):
        into[i].wait()
        out[i].start()
    for copy in out:
        copy.wait()


def per_device(queries, keys, values, out_grad, ref_keys, ref_values, frame_weight):
    hbm = pl.BlockSpec(memory_space=pl.ANY)
    shape = jax.ShapeDtypeStruct
    vmem, dma = pltpu.VMEM, pltpu.SemaphoreType.DMA
    out_shape = (shape((SEQ, WIDTH), BF),) * 3 + (shape((16, WIDTH), F32),) * 2
    grads = pl.pallas_call(
        kernel,
        name="joint_attention_grads",
        out_shape=out_shape,
        in_specs=[hbm] * 7,
        out_specs=[hbm] * 5,
        scratch_shapes=[
            vmem((4, SEQ, WIDTH), BF),
            vmem((2, 2, 4, 2, 4, 32, PAIR), BF),
            vmem((2, 2, 2 * SEQ, PAIR), BF),
            vmem((2, 2, PAIR, 2 * SEQ), BF),
            vmem((2, 5, SEQ, 2 * SEQ), F32),
            vmem((2, 5, SEQ, 2 * SEQ), F32),
            vmem((2, 5, SEQ, 2 * SEQ), BF),
            vmem((2, PAIR, SEQ), F32),
            vmem((2, 2, SEQ, PAIR), F32),
            vmem((3, SEQ, WIDTH), BF),
            vmem((2, 2, 4, 4, 4, 16, PAIR), BF),
            vmem((2, 2, 3, 4, 4, 16, PAIR), BF),
            vmem((2, 2, 4, 4, 16, PAIR), BF),
            vmem((2, 2, 3, 4, 16, PAIR), BF),
            vmem((2, 4, 2, 16, PAIR), BF),
            vmem((2, 3, 2, 16, PAIR), BF),
            vmem((1, 1), F32),
            vmem((4, 8, 128), F32),
            vmem((3, 3, 8, 128), F32),
            vmem((2, 16, WIDTH), F32),
            dma((9,)),
            dma((5,)),
            dma((2, 2, 3, 2)),
            dma((2, 2, 2)),
            dma((2, 2)),
            dma((2, 2)),
            dma((2, 2, 2, 3)),
            dma((2, 2, 2, 3)),
            dma((2, 2, 2, 3)),
            dma((2, 2, 2, 3)),
            dma((2, 2, 2, 3)),
            dma((2, 2, 2, 3)),
            dma((2, 3)),
            dma((2, 3)),
            dma((3, 3)),
            dma((3, 3)),
            pltpu.SemaphoreType.REGULAR((2,)),
        ],
        compiler_params=pltpu.CompilerParams(collective_id=0, has_side_effects=True, vmem_limit_bytes=62 * 2**20),
    )(
        queries,
        keys,
        values,
        out_grad,
        ref_keys.reshape(4, 32, -1),
        ref_values.reshape(4, 32, -1),
        frame_weight.reshape(1, 1),
    )
    return pl.pallas_call(
        hand_on,
        name="hand_on",
        out_shape=out_shape,
        in_specs=[hbm] * 5,
        out_specs=[hbm] * 5,
        scratch_shapes=[vmem(a.shape, a.dtype) for a in out_shape] + [dma((5,)), dma((5,))],
    )(*grads)


def solution(mesh):
    tokens = P("frame", "ref")
    return jax.shard_map(
        per_device,
        mesh=mesh,
        in_specs=(tokens, tokens, tokens, tokens, P("ref", None), P("ref", None), P("frame")),
        out_specs=(tokens,) * 5,
        check_vma=False,
    )
```

time: 57.4 us -> 46 us (0.80)
  local copies, waits for them, and re-layouts: 8.87 us -> 0 us
  Pallas kernels: 46.7 us -> 44.6 us
    unnamed x17 -> x0, local copies, waits for them, and re-layouts: 8.87 us -> none
    pallas_call x1 -> x2, Pallas kernels: 46.7 us -> 44.6 us  [the longest x1 42.8 us: per_device(): pl.pallas_call(kernel, name='joint_attention_grads', out_shape=out_shape,...]
where the time goes in v2:
time: 46 us; the launch traced here: 45.8 us
  Pallas kernels  44.6 us (97%)
  between operations  1.29 us (3%)
    pallas_call x1, Pallas kernels, per_device(): pl.pallas_call(kernel, name='joint_attention_grads', out_shape=out_shape,...  42.8 us
    pallas_call x1, Pallas kernels, per_device(): pl.pallas_call(hand_on, name='hand_on', out_shape=out_shape, in_specs=[hb...  1.78 us

profile of v2, /device:TPU:6, one launch (start us, length us, event | category | flops | bytes accessed | tf_op | source)
XLA Modules:
  0.0 45.8 jit_solution(9268756678022482667)
XLA Ops:
  1.3 42.8 %joint_attention_grads.1 = (bf16[256,256]{1,0:T(8,128)(2,1)}, bf16[256,256]{1,0:T(8,128)(2,1)}, bf16[256,256]{1,0:T(8,128)(2,1)}, f32[16,256]{1,0:T(8,128)}, f32[16,256]{1,0:T(8,128)}) custom-call(bf16[256,256]{1,0:T(8,128)(2,1)} %q_in.1, bf16[256,256]{1,0:T(8,128)(2,1)} %k_in.1, bf16[256,256]{1,0:T(8,128)(2,1)} %v_in.1, bf16[256,256]{1,0:T(8,128)(2,1)} %d_in.1, ...), custom_call_target="tpu_custom_call" | custom-call | tf_op jit(solution)/shard_map/joint_attention_grads/pallas_call | solution.py:309
  44.1 1.8 %hand_on.1 = (bf16[256,256]{1,0:T(8,128)(2,1)}, bf16[256,256]{1,0:T(8,128)(2,1)}, bf16[256,256]{1,0:T(8,128)(2,1)}, f32[16,256]{1,0:T(8,128)}, f32[16,256]{1,0:T(8,128)}) custom-call(bf16[256,256]{1,0:T(8,128)(2,1)} %get-tuple-element.10.refs_0_, bf16[256,256]{1,0:T(8,128)(2,1)} %get-tuple-element.11.refs_1_, bf16[256,256]{1,0:T(8,128)(2,1)} %get-tuple-element.12.refs_2_, ...), custom_call_target="tpu_custom_call" | custom-call | tf_op jit(solution)/shard_map/hand_on/pallas_call | solution.py:364

commit v3 on v2

v3 whole, which is shorter than its diff:
```python
import jax
import jax.numpy as jnp
from jax import lax
from jax.experimental import pallas as pl
from jax.experimental.pallas import tpu as pltpu
from jax.sharding import PartitionSpec as P

F32, BF = jnp.float32, jnp.bfloat16
MESH = pl.DeviceIdType.MESH
SCALE = 0.125
EXP2_SCALE = SCALE * 1.4426950408889634
SEQ, WIDTH, PAIR = 256, 256, 128
FRAMES = 64
KEY, VALUE = 0, 1


def dot(a, b):
    return lax.dot_general(a, b, (((1,), (0,)), ((), ())), preferred_element_type=F32)


def fold(a):
    return jnp.sum(a.reshape(-1, 8, a.shape[-1]), axis=0)


def split_heads(p, a, stacked, across):
    a = a[:, PAIR * p : PAIR * (p + 1)]
    low = lax.broadcasted_iota(jnp.int32, (SEQ, PAIR), 1) < 64
    zero = jnp.zeros((SEQ, PAIR), BF)
    stacked[p, 0:SEQ] = jnp.where(low, a, zero)
    stacked[p, SEQ:] = jnp.where(low, zero, a)
    turned = a.T
    top = lax.broadcasted_iota(jnp.int32, (PAIR, SEQ), 0) < 64
    zero = jnp.zeros((PAIR, SEQ), BF)
    across[p, :, 0:SEQ] = jnp.where(top, turned, zero)
    across[p, :, SEQ:] = jnp.where(top, zero, turned)


def kernel(
    q_in, k_in, v_in, d_in, rk_in, rv_in, w_in,
    gq_out, gk_out, gv_out, grk_out, grv_out,
    own, refs, stacked, across, raised, gshare, gscore, gq_t, gkv,
    part, got1, part2, got2, part3, got3, own_weight, weights, weights_got,
    loc_sem, sent_sem, zr, cr, gr, r1, r2, r3, wr, hop_sem,
):
    frame, ref = lax.axis_index("frame"), lax.axis_index("ref")
    zhi, x, y = frame // 16, (frame // 4) % 4, frame % 4
    zlo, core = ref // 2, ref % 2

    def at(dx=0, dy=0, dz=0, c=core):
        z = (zhi * 4 + zlo + dz + 16) % 16
        return (((z // 4) * 4 + (x + dx) % 4) * 4 + (y + dy) % 4, (z % 4) * 2 + c)

    def signal(sem, device):
        pl.semaphore_signal(sem, inc=1, device_id=device, device_id_type=MESH)

    near = [at(c=1 - core)]
    near += [at(dz=dz, c=c) for dz in (1, -1, 2, -2) for c in (0, 1)]
    near += [at(dx=o) for o in (1, 2, 3)] + [at(dy=o) for o in (1, 2, 3)]
    barrier = pltpu.get_barrier_semaphore()
    for device in near:
        signal(barrier, device)

    def columns(r, h):
        return pl.ds(pl.multiple_of(r * WIDTH + h * PAIR, PAIR), PAIR)

    ref_in = (rk_in, rv_in)
    weight_copy = pltpu.make_async_copy(w_in, own_weight, loc_sem.at[0])
    weight_copy.start()
    for i, a in enumerate((q_in, d_in, k_in, v_in)):
        pltpu.make_async_copy(a, own.at[i], loc_sem.at[1 + i // 2]).start()
    for h in (0, 1):
        for t in (0, 1):
            pltpu.make_async_copy(ref_in[t].at[:, :, columns(ref, h)], refs.at[t, h, 0, core], loc_sem.at[3 + h]).start()

    def copied(region, sem):
        pltpu.make_async_copy(region, region, sem).wait()

    pl.semaphore_wait(barrier, len(near))
    for dz in (2, -2):
        signal(hop_sem.at[0], at(dz=dz))

    def send(src, dst, phase, recv_sem, device):
        pltpu.make_async_remote_copy(src, dst, sent_sem.at[phase], recv_sem, device_id=device, device_id_type=MESH).start()

    def arrived(region, sem):
        pltpu.make_async_remote_copy(region, region, sent_sem.at[0], sem, device_id=at(dx=1), device_id_type=MESH).wait_recv()

    def all_sent(region, phase):
        pltpu.make_async_remote_copy(region, region, sent_sem.at[phase], wr.at[0], device_id=at(dx=1), device_id_type=MESH).wait_send()

    quarter = (x, y)
    groups = ((1, 3), (3, 4))
    for h, group, hops in ((0, 1, ((2, 3),)), (1, 0, ((1, 2), (-1, 1))), (1, 1, ((2, 3),))):
        for t in (0, 1):
            for dz, place in hops:
                for c in (0, 1):
                    target = at(dz=-dz if place == 3 and t == 1 else dz, c=c)
                    here = ref_in[t].at[quarter[t], :, columns(target[1], h)]
                    send(here, refs.at[t, h, place, core, quarter[t]], 0, zr.at[h, t, group], target)
    for t in (0, 1):
        for dz, place in ((1, 2), (-1, 1)):
            for c in (0, 1):
                target = at(dz=dz, c=c)
                send(ref_in[t].at[:, :, columns(target[1], 0)], refs.at[t, 0, place, core], 0, gr.at[0, 0], target)
    weight_copy.wait()
    weight = own_weight[0]
    weights[0] = jnp.full((8, 128), weight, F32)
    for h in (0, 1):
        for t in (0, 1):
            here = ref_in[t].at[:, :, columns(zlo * 2 + 1 - core, h)]
            send(here, refs.at[t, h, 0, core], 0, cr.at[h], at(c=1 - core))
    for o in (1, 2, 3):
        send(weights.at[0], weights_got.at[0, o - 1], 2, wr.at[0], at(dx=o))

    def gather_planes(h, group):
        first, last = groups[group]
        for t in (0, 1):
            mine = refs.at[t, h, first:last, :, quarter[t]]
            arrived(mine, zr.at[h, t, group])
            for o in (1, 2, 3):
                send(mine, mine, 0, gr.at[h, group], at(dx=o) if t == 0 else at(dy=o))

    def wait_planes(h, group):
        first, last = groups[group]
        arrived(refs.at[:, h, first:last] if (h, group) == (0, 0) else refs.at[:, h, first:last, :, 0:3], gr.at[h, group])

    totals = [None, None]

    def scores(p, j, keys, values):
        e = jnp.exp2(dot(keys, across[0, p]) * EXP2_SCALE)
        g = dot(values, across[1, p])
        raised[p, j] = e
        gshare[p, j] = g
        more = (fold(e), fold(e * g))
        totals[p] = more if totals[p] is None else (totals[p][0] + more[0], totals[p][1] + more[1])

    def ref_chunk(t, p, s):
        return refs[t, p, s].reshape(SEQ, PAIR)

    def ref_scores(p, s):
        scores(p, s, ref_chunk(0, p, s), ref_chunk(1, p, s))

    def own_chunk(i, p):
        return own[i, :, PAIR * p : PAIR * (p + 1)]

    def weight_stage(stage):
        arrived(weights_got.at[stage], wr.at[stage])
        weights[stage + 1] = weights[stage] + weights_got[stage, 0] + weights_got[stage, 1] + weights_got[stage, 2]
        if stage < 2:
            for o in (1, 2, 3):
                target = at(dy=o) if stage == 0 else at(dz=4 * o)
                send(weights.at[stage + 1], weights_got.at[stage + 1, o - 1], 2, wr.at[stage + 1], target)

    copied(own.at[0:2], loc_sem.at[1])
    for p in (0, 1):
        split_heads(p, own[0], stacked.at[0], across.at[0])
        split_heads(p, own[1], stacked.at[1], across.at[1])
    copied(own.at[2:4], loc_sem.at[2])
    scores(0, 4, own_chunk(2, 0), own_chunk(3, 0))
    gather_planes(0, 1)
    gather_planes(1, 0)
    scores(1, 4, own_chunk(2, 1), own_chunk(3, 1))
    gather_planes(1, 1)
    pl.semaphore_wait(hop_sem.at[0], 2)
    for dz in (4, -4):
        signal(hop_sem.at[1], at(dz=dz))
    weight_stage(0)
    for h in (0, 1):
        copied(refs.at[:, h, 0, core], loc_sem.at[3 + h])
        arrived(refs.at[:, h, 0, 1 - core], cr.at[h])
        ref_scores(h, 0)

    def shares(p, j, norm):
        share = raised[p, j] * norm[0]
        score = (share * (gshare[p, j] - norm[1])).astype(BF)
        gscore[p, j] = score
        return dot(score, stacked[0, p]), dot(share.astype(BF), stacked[1, p])

    norms = [None, None]

    def normalise(p):
        norm = 1.0 / jnp.sum(totals[p][0], axis=0, keepdims=True)
        norms[p] = (norm, jnp.sum(totals[p][1], axis=0, keepdims=True) * norm)

    order = (2, 1, 3, 0)
    parts = (((0, 3), (3, 4)), ((0, 1), (1, 3), (3, 4)))

    def first_stage(p, group):
        first, last = parts[p][group]
        for i in range(first, last):
            step = (zhi + order[i] - zlo + 4) % 4
            place = step + (step // 2) * (5 - 2 * step)
            for t, grad in enumerate(shares(p, place, norms[p])):
                part[t, p, i] = (grad * weight).astype(BF).reshape(4, 4, 16, PAIR)

    def first_send(p, group):
        first, last = parts[p][group]
        for o in (2, 1, 3):
            for t in (0, 1):
                here = part.at[0, p, first:last, (x + o) % 4] if t == 0 else part.at[1, p, first:last, :, (y + o) % 4]
                send(here, got1.at[t, p, o - 1, first:last], 1, r1.at[p, group], at(dx=o) if t == 0 else at(dy=o))

    def total(first, got):
        return first.astype(F32) + got[0].astype(F32) + got[1].astype(F32) + got[2].astype(F32)

    def second_stage(p, group):
        first, last = parts[p][group]
        arrived(got1.at[:, p, :, first:last], r1.at[p, group])
        for t in (0, 1):
            mine = part[0, p, first:last, x] if t == 0 else part[1, p, first:last, :, y]
            part2[t, p, first:last] = total(mine, got1[t, p, :, first:last]).astype(BF)
            for o in (2, 1, 3):
                here = part2.at[t, p, first:last, (y + o) % 4 if t == 0 else (x + o) % 4]
                send(here, got2.at[t, p, o - 1, first:last], 1, r2.at[p, group], at(dy=o) if t == 0 else at(dx=o))

    def third_stage(p, group):
        first, last = parts[p][group]
        arrived(got2.at[:, p, :, first:last], r2.at[p, group])
        for t in (0, 1):
            part3[p, first:last, t] = total(part2[t, p, first:last, y if t == 0 else x], got2[t, p, :, first:last]).astype(BF)
        for i in range(first, min(last, 3)):
            send(part3.at[p, i], got3.at[p, i], 1, r3.at[p], at(dz=4 * order[i]))

    def frame_grads(p):
        gk, gv = shares(p, 4, norms[p])
        gkv[0, p] = gk
        gkv[1, p] = gv
        sums = [None, None]
        for j in range(5):
            turned = (own_chunk(2, p) if j == 4 else ref_chunk(0, p, j)).T
            for a in (0, 1):
                more = dot(turned[64 * a : 64 * (a + 1)], gscore[p, j, :, SEQ * a : SEQ * (a + 1)])
                sums[a] = more if sums[a] is None else sums[a] + more
        gq_t[p, 0:64] = sums[0]
        gq_t[p, 64:128] = sums[1]

    wait_planes(0, 0)
    ref_scores(0, 1)
    ref_scores(0, 2)
    wait_planes(0, 1)
    ref_scores(0, 3)
    normalise(0)
    first_stage(0, 0)
    first_send(0, 0)
    first_stage(0, 1)
    wait_planes(1, 0)
    ref_scores(1, 1)
    ref_scores(1, 2)
    wait_planes(1, 1)
    ref_scores(1, 3)
    normalise(1)
    first_stage(1, 0)
    first_send(1, 0)
    first_stage(1, 1)
    first_send(1, 1)
    first_send(0, 1)
    first_stage(1, 2)
    first_send(1, 2)
    pl.semaphore_wait(hop_sem.at[1], 2)
    weight_stage(1)
    second_stage(0, 0)
    second_stage(1, 0)
    second_stage(1, 1)
    third_stage(0, 0)
    third_stage(1, 0)
    second_stage(0, 1)
    second_stage(1, 2)
    third_stage(1, 1)
    frame_grads(0)
    frame_grads(1)
    third_stage(0, 1)
    third_stage(1, 2)
    weight_stage(2)
    factor = FRAMES / weights[3, 0:1, 0:1]
    own_factor = weight * factor
    for p in (0, 1):
        cols = slice(PAIR * p, PAIR * (p + 1))
        gq_out[:, cols] = (gq_t[p].T * (own_factor * SCALE)).astype(BF)
        gk_out[:, cols] = (gkv[0, p] * (own_factor * SCALE)).astype(BF)
        gv_out[:, cols] = (gkv[1, p] * own_factor).astype(BF)
    all_sent(raised.at[0, 0:2, 0:224], 0)
    all_sent(raised.at[0, 0:3, 0:168], 1)
    all_sent(weights_got, 2)
    for p in (0, 1):
        arrived(got3.at[p], r3.at[p])
        sums = total(part3[p, 3], got3[p])
        grk_out[:, PAIR * p : PAIR * (p + 1)] = sums[0] * (factor * SCALE)
        grv_out[:, PAIR * p : PAIR * (p + 1)] = sums[1] * factor


def hand_on(*refs):
    copies = [pltpu.make_async_copy(refs[i], refs[5 + i], refs[10].at[i]) for i in range(5)]
    for copy in copies:
        copy.start()
    for copy in copies:
        copy.wait()


def per_device(queries, keys, values, out_grad, ref_keys, ref_values, frame_weight):
    hbm = pl.BlockSpec(memory_space=pl.ANY)
    shape = jax.ShapeDtypeStruct
    vmem, dma = pltpu.VMEM, pltpu.SemaphoreType.DMA
    out_shape = (shape((SEQ, WIDTH), BF),) * 3 + (shape((16, WIDTH), F32),) * 2
    grads = pl.pallas_call(
        kernel,
        name="joint_attention_grads",
        out_shape=tuple(pltpu.VMEM(a.shape, a.dtype) for a in out_shape),
        in_specs=[hbm] * 7,
        out_specs=[pl.BlockSpec(memory_space=pltpu.VMEM)] * 5,
        scratch_shapes=[
            vmem((4, SEQ, WIDTH), BF),
            vmem((2, 2, 4, 2, 4, 32, PAIR), BF),
            vmem((2, 2, 2 * SEQ, PAIR), BF),
            vmem((2, 2, PAIR, 2 * SEQ), BF),
            vmem((2, 5, SEQ, 2 * SEQ), F32),
            vmem((2, 5, SEQ, 2 * SEQ), F32),
            vmem((2, 5, SEQ, 2 * SEQ), BF),
            vmem((2, PAIR, SEQ), F32),
            vmem((2, 2, SEQ, PAIR), F32),
            vmem((2, 2, 4, 4, 4, 16, PAIR), BF),
            vmem((2, 2, 3, 4, 4, 16, PAIR), BF),
            vmem((2, 2, 4, 4, 16, PAIR), BF),
            vmem((2, 2, 3, 4, 16, PAIR), BF),
            vmem((2, 4, 2, 16, PAIR), BF),
            vmem((2, 3, 2, 16, PAIR), BF),
            pltpu.SMEM((1,), F32),
            vmem((4, 8, 128), F32),
            vmem((3, 3, 8, 128), F32),
            dma((5,)),
            dma((3,)),
            dma((2, 2, 2)),
            dma((2,)),
            dma((2, 2)),
            dma((2, 3)),
            dma((2, 3)),
            dma((2,)),
            dma((3,)),
            pltpu.SemaphoreType.REGULAR((2,)),
        ],
        compiler_params=pltpu.CompilerParams(collective_id=0, has_side_effects=True, vmem_limit_bytes=62 * 2**20),
    )(
        queries,
        keys,
        values,
        out_grad,
        ref_keys.reshape(4, 32, -1),
        ref_values.reshape(4, 32, -1),
        frame_weight,
    )
    return pl.pallas_call(
        hand_on,
        name="hand_on",
        out_shape=out_shape,
        in_specs=[pl.BlockSpec(memory_space=pltpu.VMEM)] * 5,
        out_specs=[hbm] * 5,
        scratch_shapes=[dma((5,))],
        compiler_params=pltpu.CompilerParams(vmem_limit_bytes=2**20),
    )(*grads)


def solution(mesh):
    tokens = P("frame", "ref")
    return jax.shard_map(
        per_device,
        mesh=mesh,
        in_specs=(tokens, tokens, tokens, tokens, P("ref", None), P("ref", None), P("frame")),
        out_specs=(tokens,) * 5,
        check_vma=False,
    )
```

time: 46 us -> 41.4 us (0.900)
  the two profiles are of different devices: /device:TPU:6 before, /device:TPU:1 now
where the time goes in v3:
time: 41.4 us; the launch traced here: 41.3 us
  Pallas kernels  40 us (97%)
  between operations  1.29 us (3%)
    pallas_call x1, Pallas kernels, per_device(): pl.pallas_call(kernel, name='joint_attention_grads', out_shape=tuple((plt...  39.2 us

profile of v3, /device:TPU:1, one launch (start us, length us, event | category | flops | bytes accessed | tf_op | source)
XLA Modules:
  0.0 41.3 jit_solution(17796760698596428434)
XLA Ops:
  1.3 39.2 %joint_attention_grads.1 = (bf16[256,256]{1,0:T(8,128)(2,1)S(1)}, bf16[256,256]{1,0:T(8,128)(2,1)S(1)}, bf16[256,256]{1,0:T(8,128)(2,1)S(1)}, f32[16,256]{1,0:T(8,128)S(1)}, f32[16,256]{1,0:T(8,128)S(1)}) custom-call(bf16[256,256]{1,0:T(8,128)(2,1)} %q_in.1, bf16[256,256]{1,0:T(8,128)(2,1)} %k_in.1, bf16[256,256]{1,0:T(8,128)(2,1)} %v_in.1, ...), custom_call_target="tpu_custom_call" | custom-call | tf_op jit(solution)/shard_map/joint_attention_grads/pallas_call | solution.py:304
  40.5 0.8 %hand_on.1 = (bf16[256,256]{1,0:T(8,128)(2,1)}, bf16[256,256]{1,0:T(8,128)(2,1)}, bf16[256,256]{1,0:T(8,128)(2,1)}, f32[16,256]{1,0:T(8,128)}, f32[16,256]{1,0:T(8,128)}) custom-call(bf16[256,256]{1,0:T(8,128)(2,1)S(1)} %get-tuple-element.10.refs_0_, bf16[256,256]{1,0:T(8,128)(2,1)S(1)} %get-tuple-element.11.refs_1_, ...), custom_call_target="tpu_custom_call" | custom-call | tf_op jit(solution)/shard_map/hand_on/pallas_call | solution.py:350

commit v4 on v3

--- a/solution.py
+++ b/solution.py
@@ -89,19 +89,18 @@
         pltpu.make_async_remote_copy(region, region, sent_sem.at[phase], wr.at[0], device_id=at(dx=1), device_id_type=MESH).wait_send()
 
     quarter = (x, y)
-    groups = ((1, 3), (3, 4))
-    for h, group, hops in ((0, 1, ((2, 3),)), (1, 0, ((1, 2), (-1, 1))), (1, 1, ((2, 3),))):
-        for t in (0, 1):
-            for dz, place in hops:
+    for h in (0, 1):
+        for t in (0, 1):
+            for c in (0, 1):
+                target = at(dz=2 if t == 0 else -2, c=c)
+                here = ref_in[t].at[quarter[t], :, columns(target[1], h)]
+                send(here, refs.at[t, h, 3, core, quarter[t]], 0, zr.at[h, t], target)
+    for h in (0, 1):
+        for t in (0, 1):
+            for dz, place in ((1, 2), (-1, 1)):
                 for c in (0, 1):
-                    target = at(dz=-dz if place == 3 and t == 1 else dz, c=c)
-                    here = ref_in[t].at[quarter[t], :, columns(target[1], h)]
-                    send(here, refs.at[t, h, place, core, quarter[t]], 0, zr.at[h, t, group], target)
-    for t in (0, 1):
-        for dz, place in ((1, 2), (-1, 1)):
-            for c in (0, 1):
-                target = at(dz=dz, c=c)
-                send(ref_in[t].at[:, :, columns(target[1], 0)], refs.at[t, 0, place, core], 0, gr.at[0, 0], target)
+                    target = at(dz=dz, c=c)
+                    send(ref_in[t].at[:, :, columns(target[1], h)], refs.at[t, h, place, core], 0, gr.at[h, 0], target)
     weight_copy.wait()
     weight = own_weight[0]
     weights[0] = jnp.full((8, 128), weight, F32)
@@ -112,17 +111,18 @@
     for o in (1, 2, 3):
         send(weights.at[0], weights_got.at[0, o - 1], 2, wr.at[0], at(dx=o))
 
-    def gather_planes(h, group):
-        first, last = groups[group]
-        for t in (0, 1):
-            mine = refs.at[t, h, first:last, :, quarter[t]]
-            arrived(mine, zr.at[h, t, group])
-            for o in (1, 2, 3):
-                send(mine, mine, 0, gr.at[h, group], at(dx=o) if t == 0 else at(dy=o))
-
-    def wait_planes(h, group):
-        first, last = groups[group]
-        arrived(refs.at[:, h, first:last] if (h, group) == (0, 0) else refs.at[:, h, first:last, :, 0:3], gr.at[h, group])
+    def gather_planes(h):
+        for t in (0, 1):
+            mine = refs.at[t, h, 3, :, quarter[t]]
+            arrived(mine, zr.at[h, t])
+            for o in (2, 1, 3):
+                send(mine, mine, 0, gr.at[h, 1], at(dx=o) if t == 0 else at(dy=o))
+
+    def wait_adjacent(h):
+        arrived(refs.at[:, h, 1:3], gr.at[h, 0])
+
+    def wait_planes(h):
+        arrived(refs.at[:, h, 3, :, 0:3], gr.at[h, 1])
 
     totals = [None, None]
 
@@ -157,10 +157,9 @@
         split_heads(p, own[1], stacked.at[1], across.at[1])
     copied(own.at[2:4], loc_sem.at[2])
     scores(0, 4, own_chunk(2, 0), own_chunk(3, 0))
-    gather_planes(0, 1)
-    gather_planes(1, 0)
     scores(1, 4, own_chunk(2, 1), own_chunk(3, 1))
-    gather_planes(1, 1)
+    gather_planes(0)
+    gather_planes(1)
     pl.semaphore_wait(hop_sem.at[0], 2)
     for dz in (4, -4):
         signal(hop_sem.at[1], at(dz=dz))
@@ -234,20 +233,20 @@
         gq_t[p, 0:64] = sums[0]
         gq_t[p, 64:128] = sums[1]
 
-    wait_planes(0, 0)
+    wait_adjacent(0)
     ref_scores(0, 1)
     ref_scores(0, 2)
-    wait_planes(0, 1)
+    wait_planes(0)
     ref_scores(0, 3)
     normalise(0)
     first_stage(0, 0)
     first_send(0, 0)
     first_stage(0, 1)
-    wait_planes(1, 0)
+    wait_planes(1)
+    ref_scores(1, 3)
+    wait_adjacent(1)
     ref_scores(1, 1)
     ref_scores(1, 2)
-    wait_planes(1, 1)
-    ref_scores(1, 3)
     normalise(1)
     first_stage(1, 0)
     first_send(1, 0)
@@ -328,7 +327,7 @@
             vmem((3, 3, 8, 128), F32),
             dma((5,)),
             dma((3,)),
-            dma((2, 2, 2)),
+            dma((2, 2)),
             dma((2,)),
             dma((2, 2)),
             dma((2, 3)),

time: 41.4 us -> 40.9 us (0.988)
  the two profiles are of different devices: /device:TPU:1 before, /device:TPU:6 now
where the time goes in v4:
time: 40.9 us; the launch traced here: 40.4 us
  Pallas kernels  39.1 us (96%)
  between operations  1.29 us (3%)
    pallas_call x1, Pallas kernels, per_device(): pl.pallas_call(kernel, name='joint_attention_grads', out_shape=tuple((plt...  38.3 us

profile of v4, /device:TPU:6, one launch (start us, length us, event | category | flops | bytes accessed | tf_op | source)
XLA Modules:
  0.0 40.4 jit_solution(1905474455635133867)
XLA Ops:
  1.3 38.3 %joint_attention_grads.1 = (bf16[256,256]{1,0:T(8,128)(2,1)S(1)}, bf16[256,256]{1,0:T(8,128)(2,1)S(1)}, bf16[256,256]{1,0:T(8,128)(2,1)S(1)}, f32[16,256]{1,0:T(8,128)S(1)}, f32[16,256]{1,0:T(8,128)S(1)}) custom-call(bf16[256,256]{1,0:T(8,128)(2,1)} %q_in.1, bf16[256,256]{1,0:T(8,128)(2,1)} %k_in.1, bf16[256,256]{1,0:T(8,128)(2,1)} %v_in.1, ...), custom_call_target="tpu_custom_call" | custom-call | tf_op jit(solution)/shard_map/joint_attention_grads/pallas_call | solution.py:303
  39.6 0.8 %hand_on.1 = (bf16[256,256]{1,0:T(8,128)(2,1)}, bf16[256,256]{1,0:T(8,128)(2,1)}, bf16[256,256]{1,0:T(8,128)(2,1)}, f32[16,256]{1,0:T(8,128)}, f32[16,256]{1,0:T(8,128)}) custom-call(bf16[256,256]{1,0:T(8,128)(2,1)S(1)} %get-tuple-element.10.refs_0_, bf16[256,256]{1,0:T(8,128)(2,1)S(1)} %get-tuple-element.11.refs_1_, ...), custom_call_target="tpu_custom_call" | custom-call | tf_op jit(solution)/shard_map/hand_on/pallas_call | solution.py:349

commit v5 on v4

--- a/solution.py
+++ b/solution.py
@@ -182,10 +182,10 @@
         norms[p] = (norm, jnp.sum(totals[p][1], axis=0, keepdims=True) * norm)
 
     order = (2, 1, 3, 0)
-    parts = (((0, 3), (3, 4)), ((0, 1), (1, 3), (3, 4)))
+    parts = ((0, 1), (1, 3), (3, 4))
 
     def first_stage(p, group):
-        first, last = parts[p][group]
+        first, last = parts[group]
         for i in range(first, last):
             step = (zhi + order[i] - zlo + 4) % 4
             place = step + (step // 2) * (5 - 2 * step)
@@ -193,7 +193,7 @@
                 part[t, p, i] = (grad * weight).astype(BF).reshape(4, 4, 16, PAIR)
 
     def first_send(p, group):
-        first, last = parts[p][group]
+        first, last = parts[group]
         for o in (2, 1, 3):
             for t in (0, 1):
                 here = part.at[0, p, first:last, (x + o) % 4] if t == 0 else part.at[1, p, first:last, :, (y + o) % 4]
@@ -203,7 +203,7 @@
         return first.astype(F32) + got[0].astype(F32) + got[1].astype(F32) + got[2].astype(F32)
 
     def second_stage(p, group):
-        first, last = parts[p][group]
+        first, last = parts[group]
         arrived(got1.at[:, p, :, first:last], r1.at[p, group])
         for t in (0, 1):
             mine = part[0, p, first:last, x] if t == 0 else part[1, p, first:last, :, y]
@@ -213,7 +213,7 @@
                 send(here, got2.at[t, p, o - 1, first:last], 1, r2.at[p, group], at(dy=o) if t == 0 else at(dx=o))
 
     def third_stage(p, group):
-        first, last = parts[p][group]
+        first, last = parts[group]
         arrived(got2.at[:, p, :, first:last], r2.at[p, group])
         for t in (0, 1):
             part3[p, first:last, t] = total(part2[t, p, first:last, y if t == 0 else x], got2[t, p, :, first:last]).astype(BF)
@@ -242,6 +242,8 @@
     first_stage(0, 0)
     first_send(0, 0)
     first_stage(0, 1)
+    first_send(0, 1)
+    first_stage(0, 2)
     wait_planes(1)
     ref_scores(1, 3)
     wait_adjacent(1)
@@ -252,22 +254,24 @@
     first_send(1, 0)
     first_stage(1, 1)
     first_send(1, 1)
-    first_send(0, 1)
+    first_send(0, 2)
     first_stage(1, 2)
     first_send(1, 2)
     pl.semaphore_wait(hop_sem.at[1], 2)
     weight_stage(1)
     second_stage(0, 0)
+    second_stage(0, 1)
     second_stage(1, 0)
     second_stage(1, 1)
     third_stage(0, 0)
+    second_stage(0, 2)
+    second_stage(1, 2)
     third_stage(1, 0)
-    second_stage(0, 1)
-    second_stage(1, 2)
+    third_stage(0, 1)
     third_stage(1, 1)
     frame_grads(0)
     frame_grads(1)
-    third_stage(0, 1)
+    third_stage(0, 2)
     third_stage(1, 2)
     weight_stage(2)
     factor = FRAMES / weights[3, 0:1, 0:1]

time: 40.9 us -> 40.5 us (level)
  no operation moved by 1% of the time
where the time goes in v5:
time: 40.5 us; the launch traced here: 40 us
  Pallas kernels  38.7 us (96%)
  between operations  1.29 us (3%)
    pallas_call x1, Pallas kernels, per_device(): pl.pallas_call(kernel, name='joint_attention_grads', out_shape=tuple((plt...  37.9 us

profile of v5, /device:TPU:6, one launch (start us, length us, event | category | flops | bytes accessed | tf_op | source)
XLA Modules:
  0.0 40.0 jit_solution(17949523635087914028)
XLA Ops:
  1.3 37.9 %joint_attention_grads.1 = (bf16[256,256]{1,0:T(8,128)(2,1)S(1)}, bf16[256,256]{1,0:T(8,128)(2,1)S(1)}, bf16[256,256]{1,0:T(8,128)(2,1)S(1)}, f32[16,256]{1,0:T(8,128)S(1)}, f32[16,256]{1,0:T(8,128)S(1)}) custom-call(bf16[256,256]{1,0:T(8,128)(2,1)} %q_in.1, bf16[256,256]{1,0:T(8,128)(2,1)} %k_in.1, bf16[256,256]{1,0:T(8,128)(2,1)} %v_in.1, ...), custom_call_target="tpu_custom_call" | custom-call | tf_op jit(solution)/shard_map/joint_attention_grads/pallas_call | solution.py:307
  39.2 0.8 %hand_on.1 = (bf16[256,256]{1,0:T(8,128)(2,1)}, bf16[256,256]{1,0:T(8,128)(2,1)}, bf16[256,256]{1,0:T(8,128)(2,1)}, f32[16,256]{1,0:T(8,128)}, f32[16,256]{1,0:T(8,128)}) custom-call(bf16[256,256]{1,0:T(8,128)(2,1)S(1)} %get-tuple-element.10.refs_0_, bf16[256,256]{1,0:T(8,128)(2,1)S(1)} %get-tuple-element.11.refs_1_, ...), custom_call_target="tpu_custom_call" | custom-call | tf_op jit(solution)/shard_map/hand_on/pallas_call | solution.py:353

commit v6 on v5

--- a/solution.py
+++ b/solution.py
@@ -254,20 +254,20 @@
     first_send(1, 0)
     first_stage(1, 1)
     first_send(1, 1)
-    first_send(0, 2)
     first_stage(1, 2)
-    first_send(1, 2)
     pl.semaphore_wait(hop_sem.at[1], 2)
     weight_stage(1)
     second_stage(0, 0)
     second_stage(0, 1)
     second_stage(1, 0)
+    first_send(0, 2)
+    first_send(1, 2)
     second_stage(1, 1)
     third_stage(0, 0)
+    third_stage(1, 0)
+    third_stage(0, 1)
     second_stage(0, 2)
     second_stage(1, 2)
-    third_stage(1, 0)
-    third_stage(0, 1)
     third_stage(1, 1)
     frame_grads(0)
     frame_grads(1)

time: 40.5 us -> 40.4 us (level)
  no operation moved by 1% of the time
where the time goes in v6:
time: 40.4 us; the launch traced here: 40.1 us
  Pallas kernels  38.8 us (96%)
  between operations  1.29 us (3%)
    pallas_call x1, Pallas kernels, per_device(): pl.pallas_call(kernel, name='joint_attention_grads', out_shape=tuple((plt...  38.1 us

profile of v6, /device:TPU:6, one launch (start us, length us, event | category | flops | bytes accessed | tf_op | source)
XLA Modules:
  0.0 40.1 jit_solution(2281920310444359821)
XLA Ops:
  1.3 38.1 %joint_attention_grads.1 = (bf16[256,256]{1,0:T(8,128)(2,1)S(1)}, bf16[256,256]{1,0:T(8,128)(2,1)S(1)}, bf16[256,256]{1,0:T(8,128)(2,1)S(1)}, f32[16,256]{1,0:T(8,128)S(1)}, f32[16,256]{1,0:T(8,128)S(1)}) custom-call(bf16[256,256]{1,0:T(8,128)(2,1)} %q_in.1, bf16[256,256]{1,0:T(8,128)(2,1)} %k_in.1, bf16[256,256]{1,0:T(8,128)(2,1)} %v_in.1, ...), custom_call_target="tpu_custom_call" | custom-call | tf_op jit(solution)/shard_map/joint_attention_grads/pallas_call | solution.py:307
  39.3 0.8 %hand_on.1 = (bf16[256,256]{1,0:T(8,128)(2,1)}, bf16[256,256]{1,0:T(8,128)(2,1)}, bf16[256,256]{1,0:T(8,128)(2,1)}, f32[16,256]{1,0:T(8,128)}, f32[16,256]{1,0:T(8,128)}) custom-call(bf16[256,256]{1,0:T(8,128)(2,1)S(1)} %get-tuple-element.10.refs_0_, bf16[256,256]{1,0:T(8,128)(2,1)S(1)} %get-tuple-element.11.refs_1_, ...), custom_call_target="tpu_custom_call" | custom-call | tf_op jit(solution)/shard_map/hand_on/pallas_call | solution.py:353
